TPU v7x, 32 devices: a whole 2x2x4 slice. The times are simulated.
32 devices in a mesh: dp: 8 (over z, y), rows: 4 (over x, core).
Axes of the slice: x: 2, y: 2, z: 4, core: 2. Of those that a mesh axis runs over, the one named last changes fastest.
Arguments:
- images: bfloat16 [8, 48, 64, 256], P('dp', 'rows'), may hold values from -6 to 6
- kernel: bfloat16 [3, 3, 256, 256], replicated, may hold values from -0.125 to 0.125
- cotangent: bfloat16 [8, 48, 64, 256], P('dp', 'rows'), may hold values from -6 to 6
Outputs:
- output_maps: bfloat16 [8, 48, 64, 256], P('dp', 'rows')
- grad_input: bfloat16 [8, 48, 64, 256], P('dp', 'rows')
- grad_kernel: float32 [3, 3, 256, 256], P(None, None, None, 'rows')
All inputs are finite; a program needn't handle non-finite values.
Results may differ from a plain program's by a relative error of at most 0.001.
Values may be sent and summed in bfloat16 or wider, within the bound.
A program may use at most 64 MiB of HBM per device.

v0:
```python
import jax
import jax.numpy as jnp
from jax import lax
from jax.sharding import PartitionSpec as P


def padded_2(x, sides, width):
    for axis, dim in sides:
        size, length = (lax.axis_size(axis), x.shape[dim])
        up = [(i, (i + 1) % size) for i in range(size - 1)]
        down = [(j, i) for i, j in up]
        last = lax.slice_in_dim(x, length - width, length, axis=dim)
        initial = lax.slice_in_dim(x, 0, width, axis=dim)
        before = lax.ppermute(last, axis, up)
        after = lax.ppermute(initial, axis, down)
        x = jnp.concatenate([before, x, after], axis=dim)
    return x


def conv_rows(inputs, weights):
    return lax.conv_general_dilated(
        inputs,
        weights,
        (1, 1),
        ((0, 0), (1, 1)),
        dimension_numbers=("NHWC", "HWIO", "NHWC"),
        preferred_element_type=jnp.float32,
    )


def shards(images, kernel, cotangent):
    rows_dev = images.shape[1]
    columns = images.shape[2]
    wide_images = padded_2(images, (("rows", 1),), 1)
    wide_grads = padded_2(cotangent, (("rows", 1),), 1)
    flipped = jnp.transpose(kernel[::-1, ::-1], (0, 1, 3, 2))
    output_maps = conv_rows(wide_images, kernel).astype(jnp.bfloat16)
    grad_input = conv_rows(wide_grads, flipped).astype(jnp.bfloat16)
    padded = jnp.pad(wide_images, ((0, 0), (0, 0), (1, 1), (0, 0)))
    tap_rows = []
    for tap_row in range(3):
        tap_line = []
        for tap_col in range(3):
            window = padded[:, tap_row : tap_row + rows_dev, tap_col : tap_col + columns]
            tap_line.append(
                jnp.einsum("bhwc,bhwd->cd", window, cotangent, preferred_element_type=jnp.float32)
            )
        tap_rows.append(jnp.stack(tap_line))
    local_terms = jnp.stack(tap_rows)
    groups = lax.axis_size("dp")
    row_share = lax.psum_scatter(local_terms, "rows", scatter_dimension=3, tiled=True)
    summed = lax.psum(row_share, "dp")
    batch_total = images.shape[0] * groups
    return (output_maps, grad_input, summed / float(batch_total))


def solution(mesh):
    return jax.shard_map(
        shards,
        mesh=mesh,
        in_specs=(P("dp", "rows", None, None), P(), P("dp", "rows", None, None)),
        out_specs=(
            P("dp", "rows", None, None),
            P("dp", "rows", None, None),
            P(None, None, None, "rows"),
        ),
        check_vma=False,
    )
```

profile of v0, /device:TPU:0, one launch (start us, length us, event | category | flops | bytes accessed | tf_op | source)
XLA Modules:
  0.0 180.4 jit_solution(7106152800115837669)
XLA Ops:
  7.2 0.0 copy-start
  7.2 0.0 copy-start.3
  7.2 0.0 copy-start.1
  7.2 0.0 all-reduce.7.cloned.1.call-start
  7.2 0.9 fusion.67
  8.2 2.3 %collective-permute-start = (bf16[1,1,64,256]{3,2,1,0:T(8,128)(2,1)S(1)}, bf16[1,1,64,256]{3,2,1,0:T(8,128)(2,1)S(1)}, u32[]{:S(2)}, u32[]{:S(2)}) collective-permute-start(bf16[1,1,64,256]{3,2,1,0:T(8,128)(2,1)S(1)} %get-tuple-element.15), channel_id=1, source_target_pairs={{0,1},{1,2},{2,3},{4,5},{5,6},{6,7},{8,9},{9,10},{10,11},{12,13},{... | collective-permute-start | bytes 98312 | tf_op jit(solution)/shard_map/ppermute | solution.py:14
  10.5 1.3 collective-permute-start.1
  11.8 1.4 convolution_bitcast_fusion.4
  13.3 2.4 %collective-permute-done.1 = bf16[1,1,64,256]{3,2,1,0:T(8,128)(2,1)S(1)} collective-permute-done((bf16[1,1,64,256]{3,2,1,0:T(8,128)(2,1)S(1)}, bf16[1,1,64,256]{3,2,1,0:T(8,128)(2,1)S(1)}, u32[]{:S(2)}, u32[]{:S(2)}) %collective-permute-start.1) | collective-permute-done | bytes 32800 | tf_op jit(solution)/shard_map/ppermute | solution.py:15
  15.7 0.3 convolution_bitcast_fusion.3
  16.0 0.3 convolution_bitcast_fusion.5
  16.4 0.3 convolution_bitcast_fusion.6
  16.7 0.3 convolution_bitcast_fusion.8
  17.0 0.3 convolution_bitcast_fusion
  17.3 0.3 convolution_bitcast_fusion.2
  17.6 0.3 convolution_bitcast_fusion.1
  17.9 0.1 maximum_bitcast_fusion.2
  18.0 0.3 convolution_bitcast_fusion.7
  18.3 0.1 maximum_bitcast_fusion
  18.4 0.2 pad_maximum_fusion
  18.6 2.9 %copy.26 = f32[3,3,256,256]{2,1,0,3:T(4,128)} copy(f32[3,3,256,256]{3,2,1,0:T(8,128)S(1)} %pad_maximum_fusion) | data formatting | bytes 4718592 | tf_op jit(solution)/shard_map/stack | solution.py:49
  21.5 0.0 all-reduce.7.cloned.1.call-update
  21.5 0.0 all-reduce.5.cloned.1.call-start
  21.6 0.9 copy-done.2
  22.5 4.5 %collective-permute-start.2 = (bf16[1,1,64,256]{3,2,1,0:T(8,128)(2,1)S(1)}, bf16[1,1,64,256]{3,2,1,0:T(8,128)(2,1)S(1)}, u32[]{:S(2)}, u32[]{:S(2)}) collective-permute-start(bf16[1,1,64,256]{3,2,1,0:T(8,128)(2,1)S(1)} %get-tuple-element.12), channel_id=1, source_target_pairs={{0,1},{1,2},{2,3},{4,5},{5,6},{6,7},{8,9},{9,10},{10,11},{12,13},{... | collective-permute-start | bytes 98312 | tf_op jit(solution)/shard_map/ppermute | solution.py:14
  27.0 1.3 collective-permute-start.3
  28.3 0.6 dynamic-slice
  29.6 0.3 copy.30
  29.9 0.0 copy-start.7
  29.9 0.1 pad.5.clone
  29.9 0.2 copy.20
  30.1 0.4 copy-done.7
  30.6 1.2 fusion
  31.8 0.1 copy.21
  31.9 61.2 %all-reduce.7.cloned.1.call-done = f32[3,3,256,256]{2,1,0,3:T(4,128)} async-done(((f32[3,3,256,256]{2,1,0,3:T(4,128)}), f32[3,3,256,256]{2,1,0,3:T(4,128)}) %all-reduce.7.cloned.1.call-update) | async-done | bytes 2359312
  93.1 2.2 %constant_dynamic-slice_fusion = f32[3,3,256,64]{2,1,0,3:T(4,128)} fusion(f32[3,3,256,256]{2,1,0,3:T(4,128)} %all-reduce.7.cloned.1.call-done, u32[]{:T(128)S(6)} %multiply.2), kind=kLoop, calls=%fused_computation.73 | loop fusion | bytes 1179652
  95.2 0.0 all-reduce.5.cloned.1.call-update
  95.3 0.1 maximum_bitcast_fusion.3
  95.4 0.9 copy.27
  96.2 0.3 copy.31
  96.5 0.1 pad.7.clone
  96.5 0.2 copy.24
  96.8 1.2 fusion.1
  98.0 0.1 copy.25
  98.2 0.9 copy.28
  99.0 72.3 %all-reduce.5.cloned.1.call-done = f32[3,3,256,64]{2,1,0,3:T(4,128)} async-done(((f32[3,3,256,64]{2,1,0,3:T(4,128)}), f32[3,3,256,64]{2,1,0,3:T(4,128)}) %all-reduce.5.cloned.1.call-update) | async-done | bytes 589840 | tf_op jit(solution)/shard_map/psum | solution.py:52
  171.3 1.3 broadcast_multiply_fusion
  172.6 0.9 copy.29
  (21 shorter events, 0.2 us)
Async XLA Ops:
  7.2 23.0 %copy-start = (bf16[3,3,256,256]{3,2,1,0:T(8,128)(2,1)S(1)}, bf16[3,3,256,256]{3,2,1,0:T(8,128)(2,1)}, u32[]{:S(2)}) copy-start(bf16[3,3,256,256]{3,2,1,0:T(8,128)(2,1)} %param.4) | copy-start | bytes 3538948
  7.2 6.1 %copy-start.3 = (bf16[1,12,64,256]{3,2,1,0:T(8,128)(2,1)S(1)}, bf16[1,12,64,256]{3,2,1,0:T(8,128)(2,1)}, u32[]{:S(2)}) copy-start(bf16[1,12,64,256]{3,2,1,0:T(8,128)(2,1)} %param.3) | copy-start | bytes 1179652
  7.2 8.5 %copy-start.1 = (bf16[1,12,64,256]{3,2,1,0:T(8,128)(2,1)S(1)}, bf16[1,12,64,256]{3,2,1,0:T(8,128)(2,1)}, u32[]{:S(2)}) copy-start(bf16[1,12,64,256]{3,2,1,0:T(8,128)(2,1)} %param.5) | copy-start | bytes 1179652
  7.2 85.9 %all-reduce.7.cloned.1.call-start = ((), (), s32[]{:S(2)}) async-start(), calls=%async_computation.1 | async-start | bytes 6291456
  8.2 5.1 %collective-permute-start = (bf16[1,1,64,256]{3,2,1,0:T(8,128)(2,1)S(1)}, bf16[1,1,64,256]{3,2,1,0:T(8,128)(2,1)S(1)}, u32[]{:S(2)}, u32[]{:S(2)}) collective-permute-start(bf16[1,1,64,256]{3,2,1,0:T(8,128)(2,1)S(1)} %get-tuple-element.15), channel_id=1, source_target_pairs={{0,1},{1,2},{2,3},{4,5},{5,6},{6,7},{8,9},{9,10},{10,11},{12,13},{... | collective-permute-start | bytes 98312 | tf_op jit(solution)/shard_map/ppermute | solution.py:14
  10.5 5.2 %collective-permute-start.1 = (bf16[1,1,64,256]{3,2,1,0:T(8,128)(2,1)S(1)}, bf16[1,1,64,256]{3,2,1,0:T(8,128)(2,1)S(1)}, u32[]{:S(2)}, u32[]{:S(2)}) collective-permute-start(bf16[1,1,64,256]{3,2,1,0:T(8,128)(2,1)S(1)} %get-tuple-element.14), channel_id=1, source_target_pairs={{1,0},{2,1},{3,2},{5,4},{6,5},{7,6},{9,8},{10,9},{11,10},{13,12},{... | collective-permute-start | bytes 98312 | tf_op jit(solution)/shard_map/ppermute | solution.py:15
  15.7 1.6 copy-start.4
  21.5 1.0 copy-start.2
  21.5 6.8 %copy-start.6 = (u32[32]{0:T(128)S(1)}, u32[32]{0:T(128)}, u32[]{:S(2)}) copy-start(u32[32]{0:T(128)} %constant.22) | copy-start | bytes 388
  21.5 8.1 %copy-start.5 = (bf16[1,14,64,256]{3,2,1,0:T(8,128)(2,1)S(1)}, bf16[1,14,64,256]{3,2,1,0:T(8,128)(2,1)}, u32[]{:S(2)}) copy-start(bf16[1,14,64,256]{3,2,1,0:T(8,128)(2,1)} %copy-done.4) | copy-start | bytes 1376260
  21.5 149.8 %all-reduce.5.cloned.1.call-start = ((), (), s32[]{:S(2)}) async-start(), calls=%async_computation | async-start | bytes 1572864 | tf_op jit(solution)/shard_map/psum | solution.py:52
  22.5 72.8 %collective-permute-start.2 = (bf16[1,1,64,256]{3,2,1,0:T(8,128)(2,1)S(1)}, bf16[1,1,64,256]{3,2,1,0:T(8,128)(2,1)S(1)}, u32[]{:S(2)}, u32[]{:S(2)}) collective-permute-start(bf16[1,1,64,256]{3,2,1,0:T(8,128)(2,1)S(1)} %get-tuple-element.12), channel_id=1, source_target_pairs={{0,1},{1,2},{2,3},{4,5},{5,6},{6,7},{8,9},{9,10},{10,11},{12,13},{... | collective-permute-start | bytes 98312 | tf_op jit(solution)/shard_map/ppermute | solution.py:14
  27.0 68.3 %collective-permute-start.3 = (bf16[1,1,64,256]{3,2,1,0:T(8,128)(2,1)S(1)}, bf16[1,1,64,256]{3,2,1,0:T(8,128)(2,1)S(1)}, u32[]{:S(2)}, u32[]{:S(2)}) collective-permute-start(bf16[1,1,64,256]{3,2,1,0:T(8,128)(2,1)S(1)} %get-tuple-element.13), channel_id=1, source_target_pairs={{1,0},{2,1},{3,2},{5,4},{6,5},{7,6},{9,8},{10,9},{11,10},{13,12},{... | collective-permute-start | bytes 98312 | tf_op jit(solution)/shard_map/ppermute | solution.py:15
  29.9 0.7 copy-start.7
Sparse Core Ops, SparseCore 0:
  21.6 71.3 all-reduce.6
  96.5 74.8 all-reduce.4
where the time goes:
time: 181 us; the launch traced here: 180 us
  waiting for transfers between devices  136 us (75%)
  between operations  15 us (8%)
  local copies, waits for them, and re-layouts  11.9 us (7%)
  starting transfers between devices  9.53 us (5%)
  matrix products  6.31 us (3%)
    psum x1, waiting for transfers between devices, shards(): summed = lax.psum(row_share, 'dp')  72.3 us
    unnamed x3, waiting for transfers between devices  61.2 us
    unnamed x25, local copies, waits for them, and re-layouts  7.31 us
    ppermute x2, starting transfers between devices, padded_2(): before = lax.ppermute(last, axis, up)  6.87 us
    dot_general x9, matrix products, shards(): jnp.einsum('bhwc,bhwd->cd', window, cotangent, preferred_element_type=jnp...  3.87 us
  transfers between devices with their start and end apart: 6, of which 3 were waited for; matrix products, arithmetic and copies ran while one was open for 5% of the time, Pallas kernels for 0%

commit v1 on v0

v1 whole, which is shorter than its diff:
```python
import functools

import jax
import jax.numpy as jnp
from jax import lax
from jax.experimental import pallas as pl
from jax.experimental.pallas import tpu as pltpu
from jax.sharding import PartitionSpec as P

MESH = pl.DeviceIdType.MESH
SUB = 8
TAP_ORDER = (1, 0, 2)


def bits_of(size):
    return size.bit_length() - 1


def plan(rows_size, groups, pieces):
    steps = [("rows", bit, True) for bit in reversed(range(1, bits_of(rows_size)))]
    left = pieces
    for bit in range(bits_of(groups)):
        split = left > 1
        steps.append(("dp", bit, split))
        left = left // 2 if split else left
    return steps


def body(
    dims,
    img_ref, ker_ref, cot_ref,
    out_ref, gin_ref, gk_ref,
    wide_img, wide_cot, cot_t, halo, acc, first, work, fin, *rest,
):
    rows_size, groups, rows_dev, cols, chan, steps = dims
    landing = rest[: len(steps)]
    bar_less = rest[len(steps):]
    halo_send, halo_recv, send_sem, recv_sem = bar_less
    pixels = rows_dev * cols
    pieces = chan // rows_size // SUB
    width = 3 * chan
    r = lax.axis_index("rows")
    g = lax.axis_index("dp")
    right = lax.rem(r + 1, rows_size)
    left = lax.rem(r + rows_size - 1, rows_size)

    def flip(axis, bit):
        me = r if axis == "rows" else g
        mine = lax.rem(me // (1 << bit), 2)
        return mine, {axis: me + (1 - 2 * mine) * (1 << bit)}

    core, core_peer = flip("rows", 0)
    barrier = pltpu.get_barrier_semaphore()
    greeted = [{"rows": right}, {"rows": left}, core_peer]
    greeted += [flip(axis, bit)[1] for axis, bit, _ in steps]
    for peer in greeted:
        pl.semaphore_signal(barrier, inc=1, device_id=peer, device_id_type=MESH)

    column = lax.broadcasted_iota(jnp.int32, (cols, chan), 0)

    def widen(dst, slot, value):
        full = value.astype(jnp.float32)
        before = jnp.where(column == 0, 0.0, pltpu.roll(full, 1, 0))
        after = jnp.where(column == cols - 1, 0.0, pltpu.roll(full, cols - 1, 0))
        at = pl.ds(pl.multiple_of(slot * cols, cols), cols)
        dst[at, 0:chan] = before.astype(jnp.bfloat16)
        dst[at, chan : 2 * chan] = value
        dst[at, 2 * chan :] = after.astype(jnp.bfloat16)

    def widen_rows(dst, src):
        def one(i, carry):
            widen(dst, i + 1, src[pl.ds(pl.multiple_of(i * cols, cols), cols), :])
            return carry

        lax.fori_loop(0, rows_dev, one, 0)

    pl.semaphore_wait(barrier, len(greeted))
    halos = []
    for k, (src, at, to) in enumerate((
        (img_ref, pixels - cols, right), (img_ref, 0, left),
        (cot_ref, pixels - cols, right), (cot_ref, 0, left),
    )):
        halos.append(pltpu.make_async_remote_copy(
            src_ref=src.at[pl.ds(at, cols)], dst_ref=halo.at[k],
            send_sem=halo_send.at[k], recv_sem=halo_recv.at[k],
            device_id={"rows": to}, device_id_type=MESH,
        ))
        halos[-1].start()

    cot_t[...] = jnp.transpose(cot_ref[...])
    widen_rows(wide_img, img_ref)

    def edges(dst, k):
        halos[k].wait_recv()
        halos[k + 1].wait_recv()
        zero = jnp.zeros((cols, chan), jnp.bfloat16)
        widen(dst, 0, jnp.where(r > 0, halo[k], zero))
        widen(dst, rows_dev + 1, jnp.where(r < rows_size - 1, halo[k + 1], zero))

    sent = []

    def send(src, dst, c, k, peer):
        copy = pltpu.make_async_remote_copy(
            src_ref=src, dst_ref=dst, send_sem=send_sem.at[c, k],
            recv_sem=recv_sem.at[c, k], device_id=peer, device_id_type=MESH,
        )
        copy.start()
        return copy

    def chunk(c):
        tap = TAP_ORDER[c]
        for b in range(3):
            part = jnp.dot(
                cot_t[...],
                wide_img[tap * cols : tap * cols + pixels, b * chan : (b + 1) * chan],
                preferred_element_type=jnp.float32,
            )
            acc[c, :, :, :, :, b * chan : (b + 1) * chan] = part.reshape(
                rows_size // 2, 2, pieces, SUB, chan)
        copy = send(acc.at[c, :, 1 - core], first.at[c], c, 0, core_peer)
        sent.append(copy)
        yield
        copy.wait_recv()
        work[c] = acc[c, :, core] + first[c]
        q0, nq, p0, np_ = 0, rows_size // 2, 0, pieces
        undo = []
        for k, (axis, bit, split) in enumerate(steps):
            mine, peer = flip(axis, bit)
            sq, sp = q0, p0
            if axis == "rows":
                nq //= 2
                q0, sq = q0 + mine * nq, q0 + (1 - mine) * nq
            elif split:
                np_ //= 2
                p0, sp = p0 + mine * np_, p0 + (1 - mine) * np_
                undo.append((mine, peer))
            copy = send(
                work.at[c, pl.ds(sq, nq), pl.ds(sp, np_)], landing[k].at[c], c, k + 1, peer)
            yield
            copy.wait_recv()
            if axis == "dp" and not split:
                copy.wait_send()
            else:
                sent.append(copy)
            keep = (c, pl.ds(q0, nq), pl.ds(p0, np_))
            work[keep] = work[keep] + landing[k][c]
        fin[c, pl.ds(p0, np_)] = work[c, q0, pl.ds(p0, np_)]
        for k, (mine, peer) in enumerate(reversed(undo)):
            at = fin.at[c, pl.ds(p0, np_)]
            copy = send(at, at, c, 1 + len(steps) + k, peer)
            sent.append(copy)
            yield
            copy.wait_recv()
            p0 = p0 - mine * np_
            np_ *= 2
        gk_ref[tap] = fin[c].reshape(pieces * SUB, width)

    def forward_maps():
        block = 4 * cols if rows_dev % 4 == 0 else cols

        def one(m, carry):
            total = jnp.zeros((block, chan), jnp.float32)
            for a in range(3):
                at = pl.ds(pl.multiple_of(m * block + a * cols, cols), block)
                total += jnp.dot(wide_img[at, :], ker_ref[a], preferred_element_type=jnp.float32)
            out_ref[pl.ds(pl.multiple_of(m * block, block), block), :] = total.astype(jnp.bfloat16)
            return carry

        lax.fori_loop(0, pixels // block, one, 0)

    def backward_maps():
        block = 4 * cols if rows_dev % 4 == 0 else cols

        def one(m, carry):
            total = jnp.zeros((block, chan), jnp.float32)
            for a in range(3):
                at = pl.ds(pl.multiple_of(m * block + a * cols, cols), block)
                for b in range(3):
                    total += lax.dot_general(
                        wide_cot[at, b * chan : (b + 1) * chan],
                        ker_ref[2 - a, (2 - b) * chan : (3 - b) * chan, :],
                        (((1,), (1,)), ((), ())),
                        preferred_element_type=jnp.float32,
                    )
            gin_ref[pl.ds(pl.multiple_of(m * block, block), block), :] = total.astype(jnp.bfloat16)
            return carry

        lax.fori_loop(0, pixels // block, one, 0)

    chunks = [chunk(c) for c in range(3)]
    next(chunks[0])
    edges(wide_img, 0)
    next(chunks[1])
    next(chunks[2])
    for one in chunks:
        next(one)
    forward_maps()
    next(chunks[0])
    widen_rows(wide_cot, cot_ref)
    edges(wide_cot, 2)
    backward_maps()
    next(chunks[1])
    live = chunks
    while live:
        still = []
        for one in live:
            if next(one, live) is not live:
                still.append(one)
        live = still
    for copy in halos + sent:
        copy.wait_send()


def shards(images, kernel, cotangent):
    rows_size, groups = lax.axis_size("rows"), lax.axis_size("dp")
    batch, rows_dev, cols, chan = images.shape
    pixels = rows_dev * cols
    share = chan // rows_size
    pieces = share // SUB
    width = 3 * chan
    steps = plan(rows_size, groups, pieces)
    landing = []
    nq, np_ = rows_size // 2, pieces
    for axis, _, split in steps:
        if axis == "rows":
            nq //= 2
        elif split:
            np_ //= 2
        landing.append(pltpu.VMEM((3, nq, np_, SUB, width), jnp.float32))
    count = 1 + len(steps) + sum(1 for axis, _, split in steps if axis == "dp" and split)
    vmem = pl.BlockSpec(memory_space=pltpu.VMEM)
    out, gin, gk = pl.pallas_call(
        functools.partial(body, (rows_size, groups, rows_dev, cols, chan, steps)),
        out_shape=(
            jax.ShapeDtypeStruct((pixels, chan), jnp.bfloat16),
            jax.ShapeDtypeStruct((pixels, chan), jnp.bfloat16),
            jax.ShapeDtypeStruct((3, share, width), jnp.float32),
        ),
        in_specs=[vmem] * 3,
        out_specs=(vmem,) * 3,
        scratch_shapes=[
            pltpu.VMEM(((rows_dev + 2) * cols, width), jnp.bfloat16),
            pltpu.VMEM(((rows_dev + 2) * cols, width), jnp.bfloat16),
            pltpu.VMEM((chan, pixels), jnp.bfloat16),
            pltpu.VMEM((4, cols, chan), jnp.bfloat16),
            pltpu.VMEM((3, rows_size // 2, 2, pieces, SUB, width), jnp.float32),
            pltpu.VMEM((3, rows_size // 2, pieces, SUB, width), jnp.float32),
            pltpu.VMEM((3, rows_size // 2, pieces, SUB, width), jnp.float32),
            pltpu.VMEM((3, pieces, SUB, width), jnp.float32),
            *landing,
            pltpu.SemaphoreType.DMA((4,)),
            pltpu.SemaphoreType.DMA((4,)),
            pltpu.SemaphoreType.DMA((3, count)),
            pltpu.SemaphoreType.DMA((3, count)),
        ],
        compiler_params=pltpu.CompilerParams(
            collective_id=0, has_side_effects=True, vmem_limit_bytes=40 * 2**20),
        cost_estimate=pl.CostEstimate(
            flops=6 * 9 * pixels * chan * chan, bytes_accessed=6 * 2**20, transcendentals=0),
    )(
        images.reshape(pixels, chan),
        kernel.reshape(3, 3 * chan, chan),
        cotangent.reshape(pixels, chan),
    )
    summed = jnp.transpose(gk.reshape(3, share, 3, chan), (0, 2, 3, 1))
    batch_total = batch * groups
    return (out.reshape(images.shape), gin.reshape(images.shape), summed / float(batch_total))


def solution(mesh):
    return jax.shard_map(
        shards,
        mesh=mesh,
        in_specs=(P("dp", "rows", None, None), P(), P("dp", "rows", None, None)),
        out_specs=(
            P("dp", "rows", None, None),
            P("dp", "rows", None, None),
            P(None, None, None, "rows"),
        ),
        check_vma=False,
    )
```

time: 181 us -> 51.9 us (0.29)
  waiting for transfers between devices: 136 us -> 0 us
  Pallas kernels: 0 us -> 45 us
  between operations: 15 us -> 0.67 us
  starting transfers between devices: 9.53 us -> 0 us
  matrix products: 6.31 us -> 0 us
  local copies, waits for them, and re-layouts: 11.9 us -> 5.98 us
    psum x1 -> x0, waiting for transfers between devices: 72.3 us -> none  [shards(): summed = lax.psum(row_share, 'dp')]
    unnamed x3 -> x0, waiting for transfers between devices: 61.2 us -> none
    pallas_call x0 -> x1, Pallas kernels: none -> 45 us  [shards(): pl.pallas_call(functools.partial(body, (rows_size, groups, rows_dev, cols...]
    ppermute x4 -> x0, starting transfers between devices: 9.45 us -> none  [the longest x2 6.87 us: padded_2(): before = lax.ppermute(last, axis, up)]
    dot_general x9 -> x0, matrix products: 3.87 us -> none  [shards(): jnp.einsum('bhwc,bhwd->cd', window, cotangent, preferred_element_type=jnp...]
    another operation x1 -> x0, local copies, waits for them, and re-layouts: 2.91 us -> none  [shards(): local_terms = jnp.stack(tap_rows)]
    conv_general_dilated x2 -> x0, matrix products: 2.44 us -> none  [conv_rows(): lax.conv_general_dilated(inputs, weights, (1, 1), ((0, 0), (1, 1)), dimen...]
    ppermute x4 -> x0, waiting for transfers between devices: 2.42 us -> none  [the longest x2 2.42 us: padded_2(): after = lax.ppermute(initial, axis, down)]
  transfers between devices with their start and end apart: 6 -> 0, of which waited for: 3 -> 0; matrix products, arithmetic and copies ran while one was open for 5% -> 0% of each run, Pallas kernels for 0% -> 0%
where the time goes in v1:
time: 51.9 us; the launch traced here: 51.7 us
  Pallas kernels  45 us (87%)
  local copies, waits for them, and re-layouts  5.98 us (12%)
  between operations  0.67 us (1%)
    pallas_call x1, Pallas kernels, shards(): pl.pallas_call(functools.partial(body, (rows_size, groups, rows_dev, cols...  45 us
    unnamed x9, local copies, waits for them, and re-layouts  5.66 us

profile of v1, /device:TPU:0, one launch (start us, length us, event | category | flops | bytes accessed | tf_op | source)
XLA Modules:
  0.0 51.7 jit_solution(10360978541715848415)
XLA Ops:
  0.6 0.0 copy-start
  0.6 1.3 %copy-done = bf16[3,3,256,256]{3,2,1,0:T(8,128)(2,1)S(1)} copy-done((bf16[3,3,256,256]{3,2,1,0:T(8,128)(2,1)S(1)}, bf16[3,3,256,256]{3,2,1,0:T(8,128)(2,1)}, u32[]{:S(2)}) %copy-start) | copy-done | bytes 1179672
  1.9 0.0 copy-start.1
  1.9 1.0 %copy-done.1 = bf16[1,12,64,256]{3,2,1,0:T(8,128)(2,1)S(1)} copy-done((bf16[1,12,64,256]{3,2,1,0:T(8,128)(2,1)S(1)}, bf16[1,12,64,256]{3,2,1,0:T(8,128)(2,1)}, u32[]{:S(2)}) %copy-start.1) | copy-done | bytes 393240
  2.9 0.0 copy-start.2
  2.9 1.0 %copy-done.2 = bf16[1,12,64,256]{3,2,1,0:T(8,128)(2,1)S(1)} copy-done((bf16[1,12,64,256]{3,2,1,0:T(8,128)(2,1)S(1)}, bf16[1,12,64,256]{3,2,1,0:T(8,128)(2,1)}, u32[]{:S(2)}) %copy-start.2) | copy-done | bytes 393240
  3.9 45.0 %shard_map.58 = (bf16[768,256]{1,0:T(8,128)(2,1)S(1)}, bf16[768,256]{1,0:T(8,128)(2,1)S(1)}, f32[3,64,768]{2,1,0:T(8,128)S(1)}) custom-call(bf16[768,256]{1,0:T(8,128)(2,1)S(1)} %bitcast.9, bf16[3,768,256]{2,1,0:T(8,128)(2,1)S(1)} %bitcast.8, bf16[768,256]{1,0:T(8,128)(2,1)S(1)} %bitcast.10), custom_call_target="tpu_custom_call" | custom-call | flops 2717908992 | bytes 6291456 | tf_op jit(solution)/shard_map/pallas_call | solution.py:232
  49.0 0.3 div.12
  49.3 0.9 %copy.7 = f32[3,3,256,64]{2,3,1,0:T(8,128)} copy(f32[3,3,256,64]{2,1,3,0:T(4,128)S(1)} %bitcast.11) | data formatting | bytes 1179648
  50.2 0.7 %copy.10 = bf16[1,12,64,256]{3,2,1,0:T(8,128)(2,1)} copy(bf16[1,12,64,256]{3,2,1,0:T(8,128)(2,1)S(1)} %bitcast.7) | data formatting | bytes 786432
  51.0 0.7 %copy.11 = bf16[1,12,64,256]{3,2,1,0:T(8,128)(2,1)} copy(bf16[1,12,64,256]{3,2,1,0:T(8,128)(2,1)S(1)} %bitcast.6) | data formatting | bytes 786432
  (1 shorter events, 0.0 us)
Async XLA Ops:
  0.6 1.3 %copy-start = (bf16[3,3,256,256]{3,2,1,0:T(8,128)(2,1)S(1)}, bf16[3,3,256,256]{3,2,1,0:T(8,128)(2,1)}, u32[]{:S(2)}) copy-start(bf16[3,3,256,256]{3,2,1,0:T(8,128)(2,1)} %param.4) | copy-start | bytes 3538948
  1.9 1.0 %copy-start.1 = (bf16[1,12,64,256]{3,2,1,0:T(8,128)(2,1)S(1)}, bf16[1,12,64,256]{3,2,1,0:T(8,128)(2,1)}, u32[]{:S(2)}) copy-start(bf16[1,12,64,256]{3,2,1,0:T(8,128)(2,1)} %param.3) | copy-start | bytes 1179652
  2.9 1.0 %copy-start.2 = (bf16[1,12,64,256]{3,2,1,0:T(8,128)(2,1)S(1)}, bf16[1,12,64,256]{3,2,1,0:T(8,128)(2,1)}, u32[]{:S(2)}) copy-start(bf16[1,12,64,256]{3,2,1,0:T(8,128)(2,1)} %param.5) | copy-start | bytes 1179652

commit v2 on v1

v2 whole, which is shorter than its diff:
```python
import functools

import jax
import jax.numpy as jnp
from jax import lax
from jax.experimental import pallas as pl
from jax.experimental.pallas import tpu as pltpu
from jax.sharding import PartitionSpec as P

MESH = pl.DeviceIdType.MESH
SUB = 8
TAP_ORDER = (1, 0, 2)
GAP = 3


def bits_of(size):
    return size.bit_length() - 1


def plan(rows_size, groups, pieces):
    steps = [("rows", bit, 2, True) for bit in reversed(range(1, bits_of(rows_size)))]
    left, bit = pieces, 0
    while bit < bits_of(groups):
        several = bit > 0 and left % 4 == 0 and bit + 2 <= bits_of(groups)
        members = 4 if several else 2
        split = left % members == 0
        steps.append(("dp", bit, members, split))
        left = left // members if split else left
        bit += bits_of(members)
    return steps


def body(
    dims,
    img_hbm, ker_hbm, cot_hbm,
    out_hbm, gin_hbm, gk_hbm,
    out_ref, gin_ref, img_ref, ker_ref, cot_ref, wide_img, wide_cot, cot_t, halo, acc, first, work, fin, *rest,
):
    rows_size, groups, rows_dev, cols, chan, steps = dims
    landing = rest[: len(steps)]
    load_sem, store_sem, tap_sem, halo_send, halo_recv, send_sem, recv_sem = rest[len(steps):]
    pixels = rows_dev * cols
    pieces = chan // rows_size // SUB
    r = lax.axis_index("rows")
    g = lax.axis_index("dp")
    right = lax.rem(r + 1, rows_size)
    left = lax.rem(r + rows_size - 1, rows_size)

    loads = [
        pltpu.make_async_copy(src, dst, load_sem.at[k])
        for k, (src, dst) in enumerate(
            ((img_hbm, img_ref), (cot_hbm, cot_ref), (ker_hbm, ker_ref)))
    ]
    for load in loads:
        load.start()

    def mates(axis, bit, members):
        me = r if axis == "rows" else g
        mine = lax.rem(me // (1 << bit), members)
        others = []
        for k in range(1, members):
            place = lax.rem(mine + k, members)
            others.append((place, {axis: me + (place - mine) * (1 << bit)}))
        return mine, others

    core, ((_, core_peer),) = mates("rows", 0, 2)
    barrier = pltpu.get_barrier_semaphore()
    greeted = [{"rows": right}, {"rows": left}, core_peer]
    greeted += [peer for step in steps for _, peer in mates(*step[:3])[1]]
    for peer in greeted:
        pl.semaphore_signal(barrier, inc=1, device_id=peer, device_id_type=MESH)

    column = lax.broadcasted_iota(jnp.int32, (cols, chan), 0)

    def widen(dst, slot, value):
        full = value.astype(jnp.float32)
        before = jnp.where(column == 0, 0.0, pltpu.roll(full, 1, 0))
        after = jnp.where(column == cols - 1, 0.0, pltpu.roll(full, cols - 1, 0))
        at = pl.ds(pl.multiple_of(slot * cols, cols), cols)
        dst[at, 0:chan] = before.astype(jnp.bfloat16)
        dst[at, chan : 2 * chan] = value
        dst[at, 2 * chan :] = after.astype(jnp.bfloat16)

    def widen_rows(dst, src):
        def one(i, carry):
            widen(dst, i + 1, src[pl.ds(pl.multiple_of(i * cols, cols), cols), :])
            return carry

        lax.fori_loop(0, rows_dev, one, 0)

    loads[0].wait()
    widen_rows(wide_img, img_ref)
    loads[1].wait()
    cot_t[...] = jnp.transpose(cot_ref[...])

    pl.semaphore_wait(barrier, len(greeted))
    halos = []
    for k, (src, at, to) in enumerate((
        (img_ref, pixels - cols, right), (img_ref, 0, left),
        (cot_ref, pixels - cols, right), (cot_ref, 0, left),
    )):
        halos.append(pltpu.make_async_remote_copy(
            src_ref=src.at[pl.ds(at, cols)], dst_ref=halo.at[k],
            send_sem=halo_send.at[k], recv_sem=halo_recv.at[k],
            device_id={"rows": to}, device_id_type=MESH,
        ))
        halos[-1].start()

    def edges(dst, k):
        halos[k].wait_recv()
        halos[k + 1].wait_recv()
        zero = jnp.zeros((cols, chan), jnp.bfloat16)
        widen(dst, 0, jnp.where(r > 0, halo[k], zero))
        widen(dst, rows_dev + 1, jnp.where(r < rows_size - 1, halo[k + 1], zero))

    sent, stores = [], []

    def store(src, dst, sem):
        stores.append(pltpu.make_async_copy(src, dst, sem))
        stores[-1].start()

    def send(src, dst, c, k, peer):
        copy = pltpu.make_async_remote_copy(
            src_ref=src, dst_ref=dst, send_sem=send_sem.at[c, k],
            recv_sem=recv_sem.at[c, k], device_id=peer, device_id_type=MESH,
        )
        copy.start()
        return copy

    def chunk(c):
        tap, b = TAP_ORDER[c // 3], c % 3
        part = jnp.dot(
            cot_t[...],
            wide_img[tap * cols : tap * cols + pixels, b * chan : (b + 1) * chan],
            preferred_element_type=jnp.float32,
        )
        acc[c] = part.reshape(rows_size // 2, 2, pieces, SUB, chan)
        copy = send(acc.at[c, :, 1 - core], first.at[c], c, 0, core_peer)
        sent.append(copy)
        yield
        copy.wait_recv()
        work[c] = acc[c, :, core] + first[c]
        q0, nq, p0, np_ = 0, rows_size // 2, 0, pieces
        undo = []
        sem = 1
        for k, (axis, bit, members, split) in enumerate(steps):
            mine, others = mates(axis, bit, members)
            qs, ps = q0, p0
            if axis == "rows":
                nq //= members
                q0 = qs + mine * nq
            elif split:
                np_ //= members
                p0 = ps + mine * np_
                undo.append((mine, members, others))
            copies = []
            for i, (place, peer) in enumerate(others):
                sq = qs + place * nq if axis == "rows" else q0
                sp = ps + place * np_ if axis == "dp" and split else p0
                copies.append(send(
                    work.at[c, pl.ds(sq, nq), pl.ds(sp, np_)], landing[k].at[c, i],
                    c, sem, peer))
                sem += 1
            yield
            keep = (c, pl.ds(q0, nq), pl.ds(p0, np_))
            total = work[keep]
            for i, copy in enumerate(copies):
                copy.wait_recv()
                total = total + landing[k][c, i]
                if split:
                    sent.append(copy)
                else:
                    copy.wait_send()
            work[keep] = total
        fin[c, pl.ds(p0, np_)] = work[c, q0, pl.ds(p0, np_)]
        for mine, members, others in reversed(undo):
            at = fin.at[c, pl.ds(p0, np_)]
            copies = []
            for _, peer in others:
                copies.append(send(at, at, c, sem, peer))
                sem += 1
            yield
            for copy in copies:
                copy.wait_recv()
            sent.extend(copies)
            p0 = p0 - mine * np_
            np_ *= members
        store(fin.at[c], gk_hbm.at[tap * 3 + b], tap_sem.at[c])

    block = 4 * cols if rows_dev % 4 == 0 else cols

    def forward_maps(m):
        total = jnp.zeros((block, chan), jnp.float32)
        for a in range(3):
            at = pl.ds(m * block + a * cols, block)
            total += jnp.dot(wide_img[at, :], ker_ref[a], preferred_element_type=jnp.float32)
        at = pl.ds(m * block, block)
        out_ref[at, :] = total.astype(jnp.bfloat16)
        store(out_ref.at[at], out_hbm.at[at], store_sem.at[0, m])

    def backward_maps(m):
        total = jnp.zeros((block, chan), jnp.float32)
        for a in range(3):
            at = pl.ds(m * block + a * cols, block)
            for b in range(3):
                total += lax.dot_general(
                    wide_cot[at, b * chan : (b + 1) * chan],
                    ker_ref[2 - a, (2 - b) * chan : (3 - b) * chan, :],
                    (((1,), (1,)), ((), ())),
                    preferred_element_type=jnp.float32,
                )
        at = pl.ds(m * block, block)
        gin_ref[at, :] = total.astype(jnp.bfloat16)
        store(gin_ref.at[at], gin_hbm.at[at], store_sem.at[1, m])

    def backward_inputs():
        widen_rows(wide_cot, cot_ref)
        edges(wide_cot, 2)

    asides = [functools.partial(forward_maps, m) for m in range(pixels // block)]
    asides += [backward_inputs]
    asides += [functools.partial(backward_maps, m) for m in range(pixels // block)]

    stages = 2 + len(steps) + sum(1 for s in steps if s[0] == "dp" and s[3])
    when = [0, 1] + [1 + GAP * (k - 1) for k in range(2, stages)]
    chunks = [chunk(c) for c in range(9)]
    for slot in range(9 + when[-1]):
        if slot == 3:
            edges(wide_img, 0)
            loads[2].wait()
        for k in reversed(range(stages)):
            c = slot - when[k]
            if 0 <= c < 9:
                next(chunks[c], None)
        if slot >= 3 and asides:
            asides.pop(0)()
    for aside in asides:
        aside()
    for copy in halos + sent:
        copy.wait_send()
    for copy in stores:
        copy.wait()


def shards(images, kernel, cotangent):
    rows_size, groups = lax.axis_size("rows"), lax.axis_size("dp")
    batch, rows_dev, cols, chan = images.shape
    pixels = rows_dev * cols
    share = chan // rows_size
    pieces = share // SUB
    width = 3 * chan
    steps = plan(rows_size, groups, pieces)
    landing = []
    nq, np_ = rows_size // 2, pieces
    count = 1
    for axis, _, members, split in steps:
        if axis == "rows":
            nq //= members
        elif split:
            np_ //= members
        count += (members - 1) * (2 if axis == "dp" and split else 1)
        landing.append(pltpu.VMEM((9, members - 1, nq, np_, SUB, chan), jnp.float32))
    hbm = pl.BlockSpec(memory_space=pltpu.HBM)
    out, gin, gk = pl.pallas_call(
        functools.partial(body, (rows_size, groups, rows_dev, cols, chan, steps)),
        out_shape=(
            jax.ShapeDtypeStruct((pixels, chan), jnp.bfloat16),
            jax.ShapeDtypeStruct((pixels, chan), jnp.bfloat16),
            jax.ShapeDtypeStruct((9, pieces, SUB, chan), jnp.float32),
        ),
        in_specs=[hbm] * 3,
        out_specs=(hbm,) * 3,
        scratch_shapes=[
            pltpu.VMEM((pixels, chan), jnp.bfloat16),
            pltpu.VMEM((pixels, chan), jnp.bfloat16),
            pltpu.VMEM((pixels, chan), jnp.bfloat16),
            pltpu.VMEM((3, width, chan), jnp.bfloat16),
            pltpu.VMEM((pixels, chan), jnp.bfloat16),
            pltpu.VMEM(((rows_dev + 2) * cols, width), jnp.bfloat16),
            pltpu.VMEM(((rows_dev + 2) * cols, width), jnp.bfloat16),
            pltpu.VMEM((chan, pixels), jnp.bfloat16),
            pltpu.VMEM((4, cols, chan), jnp.bfloat16),
            pltpu.VMEM((9, rows_size // 2, 2, pieces, SUB, chan), jnp.float32),
            pltpu.VMEM((9, rows_size // 2, pieces, SUB, chan), jnp.float32),
            pltpu.VMEM((9, rows_size // 2, pieces, SUB, chan), jnp.float32),
            pltpu.VMEM((9, pieces, SUB, chan), jnp.float32),
            *landing,
            pltpu.SemaphoreType.DMA((3,)),
            pltpu.SemaphoreType.DMA((2, rows_dev)),
            pltpu.SemaphoreType.DMA((9,)),
            pltpu.SemaphoreType.DMA((4,)),
            pltpu.SemaphoreType.DMA((4,)),
            pltpu.SemaphoreType.DMA((9, count)),
            pltpu.SemaphoreType.DMA((9, count)),
        ],
        compiler_params=pltpu.CompilerParams(
            collective_id=0, has_side_effects=True, vmem_limit_bytes=58 * 2**20),
        cost_estimate=pl.CostEstimate(
            flops=6 * 9 * pixels * chan * chan, bytes_accessed=6 * 2**20, transcendentals=0),
    )(
        images.reshape(pixels, chan),
        kernel.reshape(3, 3 * chan, chan),
        cotangent.reshape(pixels, chan),
    )
    summed = jnp.transpose(gk.reshape(3, 3, share, chan), (0, 1, 3, 2))
    batch_total = batch * groups
    return (out.reshape(images.shape), gin.reshape(images.shape), summed / float(batch_total))


def solution(mesh):
    return jax.shard_map(
        shards,
        mesh=mesh,
        in_specs=(P("dp", "rows", None, None), P(), P("dp", "rows", None, None)),
        out_specs=(
            P("dp", "rows", None, None),
            P("dp", "rows", None, None),
            P(None, None, None, "rows"),
        ),
        check_vma=False,
    )
```

time: 51.9 us -> 43.9 us (0.85)
  Pallas kernels: 45 us -> 39.6 us
  local copies, waits for them, and re-layouts: 5.98 us -> 1.5 us
  other arithmetic: 0.04 us -> 2 us
    pallas_call x1, Pallas kernels: 45 us -> 39.6 us  [shards(): pl.pallas_call(functools.partial(body, (rows_size, groups, rows_dev, cols...]
    unnamed x9 -> x6, local copies, waits for them, and re-layouts: 5.66 us -> 1.5 us
    div x1, other arithmetic: 0.04 us -> 2 us  [shards(): summed / float(batch_total)]
where the time goes in v2:
time: 43.9 us; the launch traced here: 43.7 us
  Pallas kernels  39.6 us (90%)
  other arithmetic  2 us (5%)
  local copies, waits for them, and re-layouts  1.5 us (3%)
  between operations  0.66 us (2%)
    pallas_call x1, Pallas kernels, shards(): pl.pallas_call(functools.partial(body, (rows_size, groups, rows_dev, cols...  39.6 us
    div x1, other arithmetic, shards(): summed / float(batch_total)  2 us
    unnamed x6, local copies, waits for them, and re-layouts  1.5 us

profile of v2, /device:TPU:0, one launch (start us, length us, event | category | flops | bytes accessed | tf_op | source)
XLA Modules:
  0.0 43.7 jit_solution(4941023292890789822)
XLA Ops:
  0.6 39.6 %shard_map.58 = (bf16[768,256]{1,0:T(8,128)(2,1)}, bf16[768,256]{1,0:T(8,128)(2,1)}, f32[9,8,8,256]{3,2,1,0:T(8,128)}) custom-call(bf16[768,256]{1,0:T(8,128)(2,1)} %bitcast.12, bf16[3,768,256]{2,1,0:T(8,128)(2,1)} %bitcast.11, bf16[768,256]{1,0:T(8,128)(2,1)} %bitcast.13), custom_call_target="tpu_custom_call" | custom-call | flops 2717908992 | bytes 6291456 | tf_op jit(solution)/shard_map/pallas_call | solution.py:264
  40.2 0.0 copy-start.1
  40.2 0.0 copy-start
  40.2 2.0 %broadcast_multiply_fusion = f32[9,8,8,256]{3,2,1,0:T(8,128)} fusion(f32[9,8,8,256]{3,2,1,0:T(8,128)} %get-tuple-element.8), kind=kLoop, calls=%fused_computation | loop fusion | flops 147456 | bytes 1179648 | tf_op jit(solution)/shard_map/div | solution.py:307
  42.2 0.0 copy-done.1
  42.3 0.7 %copy.8 = bf16[1,12,64,256]{3,2,1,0:T(8,128)(2,1)} copy(bf16[1,12,64,256]{3,2,1,0:T(8,128)(2,1)S(1)} %bitcast.10) | data formatting | bytes 786432
  43.0 0.0 copy-done
  43.0 0.7 %copy.9 = bf16[1,12,64,256]{3,2,1,0:T(8,128)(2,1)} copy(bf16[1,12,64,256]{3,2,1,0:T(8,128)(2,1)S(1)} %bitcast.9) | data formatting | bytes 786432
Async XLA Ops:
  40.2 2.0 %copy-start.1 = (bf16[768,256]{1,0:T(8,128)(2,1)S(1)}, bf16[768,256]{1,0:T(8,128)(2,1)}, u32[]{:S(2)}) copy-start(bf16[768,256]{1,0:T(8,128)(2,1)} %get-tuple-element.6) | copy-start | bytes 1179652
  40.2 2.8 %copy-start = (bf16[768,256]{1,0:T(8,128)(2,1)S(1)}, bf16[768,256]{1,0:T(8,128)(2,1)}, u32[]{:S(2)}) copy-start(bf16[768,256]{1,0:T(8,128)(2,1)} %get-tuple-element.7) | copy-start | bytes 1179652

commit v3 on v2

--- a/solution.py
+++ b/solution.py
@@ -9,7 +9,7 @@
 
 MESH = pl.DeviceIdType.MESH
 SUB = 8
-TAP_ORDER = (1, 0, 2)
+TAPS = [(a, b) for a in (1, 0, 2) for b in (1, 0, 2)]
 GAP = 3
 
 
@@ -19,14 +19,11 @@
 
 def plan(rows_size, groups, pieces):
     steps = [("rows", bit, 2, True) for bit in reversed(range(1, bits_of(rows_size)))]
-    left, bit = pieces, 0
-    while bit < bits_of(groups):
-        several = bit > 0 and left % 4 == 0 and bit + 2 <= bits_of(groups)
-        members = 4 if several else 2
-        split = left % members == 0
-        steps.append(("dp", bit, members, split))
-        left = left // members if split else left
-        bit += bits_of(members)
+    left = pieces
+    for bit in range(bits_of(groups)):
+        split = left > 1 and bit + 1 < bits_of(groups)
+        steps.append(("dp", bit, 2, split))
+        left = left // 2 if split else left
     return steps
 
 
@@ -36,7 +33,7 @@
     out_hbm, gin_hbm, gk_hbm,
     out_ref, gin_ref, img_ref, ker_ref, cot_ref, wide_img, wide_cot, cot_t, halo, acc, first, work, fin, *rest,
 ):
-    rows_size, groups, rows_dev, cols, chan, steps = dims
+    rows_size, groups, rows_dev, cols, chan, batch_total, steps = dims
     landing = rest[: len(steps)]
     load_sem, store_sem, tap_sem, halo_send, halo_recv, send_sem, recv_sem = rest[len(steps):]
     pixels = rows_dev * cols
@@ -88,11 +85,18 @@
 
         lax.fori_loop(0, rows_dev, one, 0)
 
-    loads[0].wait()
-    widen_rows(wide_img, img_ref)
     loads[1].wait()
     cot_t[...] = jnp.transpose(cot_ref[...])
-
+    loads[0].wait()
+
+    def partial(c):
+        tap, b = TAPS[c]
+        window = img_ref[...] if c == 0 else wide_img[
+            tap * cols : tap * cols + pixels, b * chan : (b + 1) * chan]
+        part = jnp.dot(cot_t[...], window, preferred_element_type=jnp.float32)
+        acc[c] = part.reshape(rows_size // 2, 2, pieces, SUB, chan)
+
+    partial(0)
     pl.semaphore_wait(barrier, len(greeted))
     halos = []
     for k, (src, at, to) in enumerate((
@@ -128,13 +132,8 @@
         return copy
 
     def chunk(c):
-        tap, b = TAP_ORDER[c // 3], c % 3
-        part = jnp.dot(
-            cot_t[...],
-            wide_img[tap * cols : tap * cols + pixels, b * chan : (b + 1) * chan],
-            preferred_element_type=jnp.float32,
-        )
-        acc[c] = part.reshape(rows_size // 2, 2, pieces, SUB, chan)
+        if c > 0:
+            partial(c)
         copy = send(acc.at[c, :, 1 - core], first.at[c], c, 0, core_peer)
         sent.append(copy)
         yield
@@ -172,7 +171,7 @@
                 else:
                     copy.wait_send()
             work[keep] = total
-        fin[c, pl.ds(p0, np_)] = work[c, q0, pl.ds(p0, np_)]
+        fin[c, pl.ds(p0, np_)] = work[c, q0, pl.ds(p0, np_)] / float(batch_total)
         for mine, members, others in reversed(undo):
             at = fin.at[c, pl.ds(p0, np_)]
             copies = []
@@ -185,7 +184,7 @@
             sent.extend(copies)
             p0 = p0 - mine * np_
             np_ *= members
-        store(fin.at[c], gk_hbm.at[tap * 3 + b], tap_sem.at[c])
+        store(fin.at[c], gk_hbm.at[TAPS[c][0] * 3 + TAPS[c][1]], tap_sem.at[c])
 
     block = 4 * cols if rows_dev % 4 == 0 else cols
 
@@ -232,6 +231,8 @@
             c = slot - when[k]
             if 0 <= c < 9:
                 next(chunks[c], None)
+        if slot == 0:
+            widen_rows(wide_img, img_ref)
         if slot >= 3 and asides:
             asides.pop(0)()
     for aside in asides:
@@ -262,7 +263,7 @@
         landing.append(pltpu.VMEM((9, members - 1, nq, np_, SUB, chan), jnp.float32))
     hbm = pl.BlockSpec(memory_space=pltpu.HBM)
     out, gin, gk = pl.pallas_call(
-        functools.partial(body, (rows_size, groups, rows_dev, cols, chan, steps)),
+        functools.partial(body, (rows_size, groups, rows_dev, cols, chan, batch * groups, steps)),
         out_shape=(
             jax.ShapeDtypeStruct((pixels, chan), jnp.bfloat16),
             jax.ShapeDtypeStruct((pixels, chan), jnp.bfloat16),
@@ -303,8 +304,7 @@
         cotangent.reshape(pixels, chan),
     )
     summed = jnp.transpose(gk.reshape(3, 3, share, chan), (0, 1, 3, 2))
-    batch_total = batch * groups
-    return (out.reshape(images.shape), gin.reshape(images.shape), summed / float(batch_total))
+    return (out.reshape(images.shape), gin.reshape(images.shape), summed)
 
 
 def solution(mesh):

time: 43.9 us -> 43.4 us (0.989)
  local copies, waits for them, and re-layouts: 1.5 us -> 4.41 us
  other arithmetic: 2 us -> 0 us
  Pallas kernels: 39.6 us -> 38.1 us
    unnamed x6 -> x5, local copies, waits for them, and re-layouts: 1.5 us -> 4.41 us
    div x1 -> x0, other arithmetic: 2 us -> none  [shards(): summed / float(batch_total)]
    pallas_call x1, Pallas kernels: 39.6 us -> 38.1 us  [shards(): pl.pallas_call(functools.partial(body, (rows_size, groups, rows_dev, cols...]
where the time goes in v3:
time: 43.4 us; the launch traced here: 43.2 us
  Pallas kernels  38.1 us (88%)
  local copies, waits for them, and re-layouts  4.41 us (10%)
  between operations  0.65 us (1%)
    pallas_call x1, Pallas kernels, shards(): pl.pallas_call(functools.partial(body, (rows_size, groups, rows_dev, cols...  38.1 us
    unnamed x5, local copies, waits for them, and re-layouts  4.41 us

profile of v3, /device:TPU:0, one launch (start us, length us, event | category | flops | bytes accessed | tf_op | source)
XLA Modules:
  0.0 43.2 jit_solution(4917219186115101236)
XLA Ops:
  0.6 38.1 %shard_map.58 = (bf16[768,256]{1,0:T(8,128)(2,1)}, bf16[768,256]{1,0:T(8,128)(2,1)}, f32[9,8,8,256]{3,2,1,0:T(8,128)}) custom-call(bf16[768,256]{1,0:T(8,128)(2,1)} %bitcast.12, bf16[3,768,256]{2,1,0:T(8,128)(2,1)} %bitcast.11, bf16[768,256]{1,0:T(8,128)(2,1)} %bitcast.13), custom_call_target="tpu_custom_call" | custom-call | flops 2717908992 | bytes 6291456 | tf_op jit(solution)/shard_map/pallas_call | solution.py:265
  38.8 0.0 copy-start
  38.8 1.8 %copy.9 = bf16[1,12,64,256]{3,2,1,0:T(8,128)(2,1)} copy(bf16[1,12,64,256]{3,2,1,0:T(8,128)(2,1)} %bitcast.10) | data formatting | bytes 786432
  40.6 1.8 %copy.10 = bf16[1,12,64,256]{3,2,1,0:T(8,128)(2,1)} copy(bf16[1,12,64,256]{3,2,1,0:T(8,128)(2,1)} %bitcast.9) | data formatting | bytes 786432
  42.4 0.0 copy-done
  42.4 0.8 %copy.11 = f32[3,3,256,64]{2,3,1,0:T(8,128)} copy(f32[3,3,256,64]{2,3,1,0:T(8,128)S(1)} %bitcast.8) | data formatting | bytes 1179648
Async XLA Ops:
  38.8 3.6 %copy-start = (f32[9,8,8,256]{3,2,1,0:T(8,128)S(1)}, f32[9,8,8,256]{3,2,1,0:T(8,128)}, u32[]{:S(2)}) copy-start(f32[9,8,8,256]{3,2,1,0:T(8,128)} %get-tuple-element.8) | copy-start | bytes 1769476
